TPU v7x, 32 devices: a whole 2x2x4 slice. The times are simulated.
32 devices in a mesh: tm: 4 (over y, x), space: 8 (over z, core).
Axes of the slice: x: 2, y: 2, z: 4, core: 2. Of those that a mesh axis runs over, the one named last changes fastest.
Arguments:
- latent_clip: bfloat16 [8, 16, 32, 256], P('tm', 'space'), may hold values from -45 to 45
- cotangent: bfloat16 [8, 16, 32, 128], P('tm', 'space'), may hold values from -6 to 6
- conv_weight: bfloat16 [6912, 128], replicated, may hold values from -0.078125 to 0.078125
- norm_gain: float32 [256], replicated, may hold values from 0.5 to 1.5
- norm_shift: float32 [256], replicated, may hold values from -2 to 2
Outputs:
- clip_grad: bfloat16 [8, 16, 32, 256], P('tm', 'space')
- weight_grad: float32 [6912, 128], P('space')
- gain_grad: float32 [256], replicated
- shift_grad: float32 [256], replicated
All inputs are finite; a program needn't handle non-finite values.
Results may differ from a plain program's by a relative error of at most 0.0029.
Values may be sent and summed in bfloat16 or wider, within the bound.
A program may use at most 64 MiB of HBM per device.

v0:
```python
import jax
import jax.numpy as jnp
from jax import lax
from jax.sharding import PartitionSpec as P

GROUPS = 32


def shifted(value, axis, steps):
    count = lax.axis_size(axis)
    leading, last = (max(0, -steps), min(count, count - steps))
    return lax.ppermute(value, axis, [(source, source + steps) for source in range(leading, last)])


def extended_2(block, sides, width):
    for axis, dim in sides:
        count = lax.axis_size(axis)
        forward = [(i, i + 1) for i in range(count - 1)]
        backward = [(target, source) for source, target in forward]
        low = lax.ppermute(
            lax.slice_in_dim(block, block.shape[dim] - width, None, axis=dim), axis, forward
        )
        high = lax.ppermute(lax.slice_in_dim(block, 0, width, axis=dim), axis, backward)
        block = jnp.concatenate([low, block, high], axis=dim)
    return block


def silu_slope(activation):
    sigma = jax.nn.sigmoid(activation)
    return sigma * (1.0 + activation * (1.0 - sigma))


def tap_block(source, anchors, frame_count, row_count, col_count):
    pieces = [
        source[
            anchor[0] : anchor[0] + frame_count,
            anchor[1] : anchor[1] + row_count,
            anchor[2] : anchor[2] + col_count,
            :,
        ]
        for anchor in anchors
    ]
    merged = jnp.concatenate(pieces, axis=-1)
    return merged.reshape(frame_count * row_count * col_count, merged.shape[-1])


def transposed(grad_pad, conv_weight, frame_count, row_count, col_count):
    out_channels = conv_weight.shape[1]
    channels = conv_weight.shape[0] // 27
    kernel = conv_weight.reshape(3, 3, 3, channels, out_channels)
    total = jnp.zeros((frame_count * row_count * col_count, channels), jnp.float32)
    for tap_time in range(3):
        anchors = [
            (2 - tap_time, 2 - tap_row, 2 - tap_col) for tap_row in range(3) for tap_col in range(3)
        ]
        tap_cols = tap_block(grad_pad, anchors, frame_count, row_count, col_count)
        flipped = jnp.transpose(kernel[tap_time], (0, 1, 3, 2)).reshape(9 * out_channels, channels)
        total = total + jnp.dot(tap_cols, flipped, preferred_element_type=jnp.float32)
    return total.reshape(frame_count, row_count, col_count, channels)


def shards(latent_clip, cotangent, conv_weight, norm_gain, norm_shift):
    frame_count, row_count, col_count, channels = latent_clip.shape
    out_channels = cotangent.shape[-1]
    width_group = channels // GROUPS
    tm_size = lax.axis_size("tm")
    space_size = lax.axis_size("space")
    group_count = frame_count * row_count * col_count * width_group * tm_size * space_size
    values = latent_clip.astype(jnp.float32).reshape(
        frame_count, row_count, col_count, GROUPS, width_group
    )
    group_mean = lax.psum(jnp.sum(values, axis=(0, 1, 2, 4)), ("tm", "space")) / group_count
    centered = values - group_mean[:, None]
    group_var = (
        lax.psum(jnp.sum(centered * centered, axis=(0, 1, 2, 4)), ("tm", "space")) / group_count
    )
    inv_std = lax.rsqrt(group_var + 1e-06)
    normed = (centered * inv_std[:, None]).reshape(frame_count, row_count, col_count, channels)
    activation = normed * norm_gain + norm_shift
    hidden = jax.nn.silu(activation).astype(jnp.bfloat16)
    ahead = shifted(cotangent, "tm", -1)
    time_source = jnp.concatenate([cotangent, ahead], axis=0)
    time_pad = (0, 0)
    cached = shifted(hidden, "tm", 1)
    extended = jnp.concatenate([cached, hidden], axis=0)
    rimmed = extended_2(extended, (("space", 1),), 1)
    padded = jnp.pad(rimmed, ((0, 0), (0, 0), (1, 1), (0, 0)))
    cell_count = frame_count * row_count * col_count
    upstream = cotangent.reshape(cell_count, out_channels)
    tap_grads = []
    for tap_time in range(3):
        anchors = [(tap_time, tap_row, tap_col) for tap_row in range(3) for tap_col in range(3)]
        tap_cols = tap_block(padded, anchors, frame_count, row_count, col_count)
        tap_grads.append(
            lax.dot_general(
                tap_cols, upstream, (((0,), (0,)), ((), ())), preferred_element_type=jnp.float32
            )
        )
    local_grad = jnp.concatenate(tap_grads, axis=0)
    space_shard = lax.psum_scatter(local_grad, "space", scatter_dimension=0, tiled=True)
    weight_grad = lax.psum(space_shard, "tm")
    grad_pad = jnp.pad(time_source, (time_pad, (2, 2), (1, 1), (0, 0)))
    spread = transposed(grad_pad, conv_weight, frame_count, row_count + 2, col_count)
    from_below = shifted(spread[:, 0], "space", -1)
    from_above = shifted(spread[:, row_count + 1], "space", 1)
    inner = spread[:, 1 : row_count + 1]
    inner = inner.at[:, row_count - 1].add(from_below)
    inner = inner.at[:, 0].add(from_above)
    activation_grad = inner * silu_slope(activation)
    gain_grad, shift_grad = lax.psum(
        (
            jnp.sum(activation_grad * normed, axis=(0, 1, 2)),
            jnp.sum(activation_grad, axis=(0, 1, 2)),
        ),
        ("tm", "space"),
    )
    first = jnp.sum((norm_gain * shift_grad).reshape(GROUPS, width_group), axis=1)
    second = jnp.sum((norm_gain * gain_grad).reshape(GROUPS, width_group), axis=1)
    scaled = (activation_grad * norm_gain).reshape(
        frame_count, row_count, col_count, GROUPS, width_group
    )
    normed_groups = normed.reshape(frame_count, row_count, col_count, GROUPS, width_group)
    clip_grad = inv_std[:, None] * (
        scaled - first[:, None] / group_count - normed_groups * second[:, None] / group_count
    )
    clip_grad = clip_grad.reshape(frame_count, row_count, col_count, channels).astype(jnp.bfloat16)
    return (clip_grad, weight_grad, gain_grad, shift_grad)


def solution(mesh):
    return jax.shard_map(
        shards,
        mesh=mesh,
        in_specs=(P("tm", "space", None, None), P("tm", "space", None, None), P(), P(), P()),
        out_specs=(P("tm", "space", None, None), P("space", None), P(), P()),
        check_vma=False,
    )
```

profile of v0, /device:TPU:0, one launch (start us, length us, event | category | flops | bytes accessed | tf_op | source)
XLA Modules:
  0.0 225.5 jit_solution(13261450040164895884)
XLA Ops:
  7.2 0.0 reduce-scatter.2.cloned.1.call-start
  7.2 0.9 convert_reduce_fusion
  8.1 0.1 reduce_sum.69
  8.2 0.1 reduce_sum.70
  8.3 1.3 collective-permute-start
  9.6 43.2 %psum.35 = f32[32]{0:T(128)S(1)} all-reduce(f32[32]{0:T(128)S(1)} %reduce_sum.70), channel_id=1, replica_groups=mesh['tm'=4,'space'=8] {'tm','space'}, use_global_device_ids=true, to_apply=%region_2.0 | all-reduce | flops 32 | bytes 256 | tf_op jit(solution)/shard_map/psum | solution.py:72
  52.8 0.1 sub.35
  52.8 0.1 sub.36
  52.9 0.9 fusion.33
  53.8 0.1 reduce_sum.72
  53.9 0.1 reduce_sum.73
  54.0 1.5 fusion.40
  55.6 41.0 %psum.36 = f32[32]{0:T(128)S(1)} all-reduce(f32[32]{0:T(128)S(1)} %reduce_sum.73), channel_id=1, replica_groups=mesh['tm'=4,'space'=8] {'tm','space'}, use_global_device_ids=true, to_apply=%region_5.6 | all-reduce | flops 32 | bytes 256 | tf_op jit(solution)/shard_map/psum | solution.py:75
  96.6 0.2 copy.15
  96.8 0.0 copy-start.1
  96.8 0.2 copy.13
  97.1 0.2 copy.14
  97.3 0.2 copy-done.1
  97.7 0.1 constant_dynamic-update-slice_fusion.25
  97.7 0.1 constant_dynamic-update-slice_fusion.24
  97.8 0.1 constant_dynamic-update-slice_fusion.23
  97.9 0.1 constant_dynamic-update-slice_fusion.22
  98.0 0.1 constant_dynamic-update-slice_fusion.21
  98.0 0.1 constant_dynamic-update-slice_fusion.20
  98.1 0.1 constant_dynamic-update-slice_fusion.19
  98.2 0.1 constant_dynamic-update-slice_fusion.18
  98.3 0.3 fusion.42
  98.6 0.3 convolution_add_fusion.1
  99.0 0.0 copy-start
  99.0 0.0 copy-start.2
  99.0 0.0 copy-start.3
  99.0 0.3 convolution_add_fusion
  99.4 1.3 collective-permute-start.1
  100.7 0.1 mul.75
  100.8 0.1 mul.76
  100.9 3.0 %collective-permute-start.2 = (f32[2,32,256]{2,1,0:T(8,128)S(1)}, f32[2,32,256]{2,1,0:T(8,128)S(1)}, u32[]{:S(2)}, u32[]{:S(2)}) collective-permute-start(f32[2,32,256]{2,1,0:T(8,128)S(1)} %get-tuple-element.53), channel_id=1, source_target_pairs={{0,1},{1,2},{2,3},{3,4},{4,5},{5,6},{6,7},{8,9},{9,10},{10,11},{11... | collective-permute-start | bytes 196616 | tf_op jit(solution)/shard_map/ppermute | solution.py:12
  103.9 0.9 collective-permute-done.2
  104.8 0.1 fusion.38
  105.0 4.2 %collective-permute-start.3 = (bf16[2,2,32,256]{3,2,1,0:T(8,128)(2,1)S(1)}, bf16[2,2,32,256]{3,2,1,0:T(8,128)(2,1)S(1)}, u32[]{:S(2)}, u32[]{:S(2)}) collective-permute-start(bf16[2,2,32,256]{3,2,1,0:T(8,128)(2,1)S(1)} %get-tuple-element.90), channel_id=1, source_target_pairs={{0,8},{8,16},{16,24},{1,9},{9,17},{17,25},{2,10},{10,18},{18,26},{... | collective-permute-start | bytes 196616 | tf_op jit(solution)/shard_map/ppermute | solution.py:12
  109.1 1.9 collective-permute-done.3
  111.1 1.4 collective-permute-start.4
  112.6 1.3 collective-permute-start.5
  113.9 4.6 %collective-permute-done.5 = bf16[4,1,32,256]{3,2,1,0:T(8,128)(2,1)S(1)} collective-permute-done((bf16[4,1,32,256]{3,2,1,0:T(8,128)(2,1)S(1)}, bf16[4,1,32,256]{3,2,1,0:T(8,128)(2,1)S(1)}, u32[]{:S(2)}, u32[]{:S(2)}) %collective-permute-start.5) | collective-permute-done | bytes 65568 | tf_op jit(solution)/shard_map/ppermute | solution.py:23
  118.4 0.1 select_maximum_fusion
  118.9 0.3 convolution_bitcast_fusion
  119.2 0.3 convolution_bitcast_fusion.2
  119.6 0.3 convolution_bitcast_fusion.1
  119.9 2.0 pad_maximum_fusion
  121.9 0.0 reduce-scatter.2.cloned.1.call-update
  122.0 0.0 all-reduce.5.cloned.1.call-start
  122.0 45.1 %all-reduce.2 = (f32[256]{0:T(256)S(1)}, f32[256]{0:T(256)S(1)}) all-reduce(f32[256]{0:T(256)S(1)} %get-tuple-element.29, f32[256]{0:T(256)S(1)} %get-tuple-element.28), channel_id=1, replica_groups=mesh['tm'=4,'space'=8] {'tm','space'}, use_global_device_ids=true, to_apply=%region_10.11 | all-reduce | flops 512 | bytes 4096 | tf_op jit(solution)/shard_map/psum | solution.py:110
  167.2 0.1 reshape.151
  167.2 0.1 reduce_sum.75
  167.4 3.1 %reduce-scatter.2.cloned.1.call-done = f32[864,128]{1,0:T(8,128)} async-done(((f32[6912,128]{1,0:T(8,128)}), f32[864,128]{1,0:T(8,128)}) %reduce-scatter.2.cloned.1.call-update) | async-done | bytes 442384 | tf_op jit(solution)/shard_map/reduce_scatter | solution.py:100
  170.5 0.0 all-reduce.5.cloned.1.call-update
  170.5 0.1 sub.40
  170.6 0.1 sub.41
  170.7 0.1 reshape.152
  170.8 0.1 reduce_sum.77
  170.9 0.1 mul.88
  171.0 0.1 mul.89
  171.1 0.7 fusion.32
  171.8 45.1 %all-reduce.5.cloned.1.call-done = f32[864,128]{1,0:T(8,128)} async-done(((f32[864,128]{1,0:T(8,128)}), f32[864,128]{1,0:T(8,128)}) %all-reduce.5.cloned.1.call-update) | async-done | bytes 442384 | tf_op jit(solution)/shard_map/psum | solution.py:101
  216.9 1.8 copy.74
  (35 shorter events, 0.4 us)
Async XLA Ops:
  7.2 163.3 %reduce-scatter.2.cloned.1.call-start = ((), (), s32[]{:S(2)}) async-start(), calls=%async_computation.1 | async-start | bytes 3981312 | tf_op jit(solution)/shard_map/reduce_scatter | solution.py:100
  8.3 89.0 %collective-permute-start = (bf16[2,2,32,128]{3,2,1,0:T(8,128)(2,1)}, bf16[2,2,32,128]{3,2,1,0:T(8,128)(2,1)S(1)}, u32[]{:S(2)}, u32[]{:S(2)}) collective-permute-start(bf16[2,2,32,128]{3,2,1,0:T(8,128)(2,1)} %param.10), channel_id=1, source_target_pairs={{8,0},{16,8},{24,16},{9,1},{17,9},{25,17},{10,2},{18,10},{26,18},{... | collective-permute-start | bytes 98312 | tf_op jit(solution)/shard_map/ppermute | solution.py:12
  96.8 0.8 copy-start.1
  99.0 5.8 %copy-start = (bf16[2,2,32,256]{3,2,1,0:T(8,128)(2,1)S(1)}, bf16[2,2,32,256]{3,2,1,0:T(8,128)(2,1)}, u32[]{:S(2)}) copy-start(bf16[2,2,32,256]{3,2,1,0:T(8,128)(2,1)} %param.9) | copy-start | bytes 196612
  99.0 5.8 %copy-start.2 = (f32[256]{0:T(256)S(1)}, f32[256]{0:T(256)}, u32[]{:S(2)}) copy-start(f32[256]{0:T(256)} %param.12) | copy-start | bytes 3076
  99.0 5.8 %copy-start.3 = (f32[256]{0:T(256)S(1)}, f32[256]{0:T(256)}, u32[]{:S(2)}) copy-start(f32[256]{0:T(256)} %param.13) | copy-start | bytes 3076
  99.4 4.5 %collective-permute-start.1 = (f32[2,32,256]{2,1,0:T(8,128)S(1)}, f32[2,32,256]{2,1,0:T(8,128)S(1)}, u32[]{:S(2)}, u32[]{:S(2)}) collective-permute-start(f32[2,32,256]{2,1,0:T(8,128)S(1)} %get-tuple-element.54), channel_id=1, source_target_pairs={{1,0},{2,1},{3,2},{4,3},{5,4},{6,5},{7,6},{9,8},{10,9},{11,10},{12... | collective-permute-start | bytes 196616 | tf_op jit(solution)/shard_map/ppermute | solution.py:12
  100.9 3.9 %collective-permute-start.2 = (f32[2,32,256]{2,1,0:T(8,128)S(1)}, f32[2,32,256]{2,1,0:T(8,128)S(1)}, u32[]{:S(2)}, u32[]{:S(2)}) collective-permute-start(f32[2,32,256]{2,1,0:T(8,128)S(1)} %get-tuple-element.53), channel_id=1, source_target_pairs={{0,1},{1,2},{2,3},{3,4},{4,5},{5,6},{6,7},{8,9},{9,10},{10,11},{11... | collective-permute-start | bytes 196616 | tf_op jit(solution)/shard_map/ppermute | solution.py:12
  105.0 6.1 %collective-permute-start.3 = (bf16[2,2,32,256]{3,2,1,0:T(8,128)(2,1)S(1)}, bf16[2,2,32,256]{3,2,1,0:T(8,128)(2,1)S(1)}, u32[]{:S(2)}, u32[]{:S(2)}) collective-permute-start(bf16[2,2,32,256]{3,2,1,0:T(8,128)(2,1)S(1)} %get-tuple-element.90), channel_id=1, source_target_pairs={{0,8},{8,16},{16,24},{1,9},{9,17},{17,25},{2,10},{10,18},{18,26},{... | collective-permute-start | bytes 196616 | tf_op jit(solution)/shard_map/ppermute | solution.py:12
  111.1 2.8 %collective-permute-start.4 = (bf16[4,1,32,256]{3,2,1,0:T(8,128)(2,1)S(1)}, bf16[4,1,32,256]{3,2,1,0:T(8,128)(2,1)S(1)}, u32[]{:S(2)}, u32[]{:S(2)}) collective-permute-start(bf16[4,1,32,256]{3,2,1,0:T(8,128)(2,1)S(1)} %get-tuple-element.88), channel_id=1, source_target_pairs={{0,1},{1,2},{2,3},{3,4},{4,5},{5,6},{6,7},{8,9},{9,10},{10,11},{11... | collective-permute-start | bytes 196616 | tf_op jit(solution)/shard_map/ppermute | solution.py:20
  112.6 5.9 %collective-permute-start.5 = (bf16[4,1,32,256]{3,2,1,0:T(8,128)(2,1)S(1)}, bf16[4,1,32,256]{3,2,1,0:T(8,128)(2,1)S(1)}, u32[]{:S(2)}, u32[]{:S(2)}) collective-permute-start(bf16[4,1,32,256]{3,2,1,0:T(8,128)(2,1)S(1)} %get-tuple-element.89), channel_id=1, source_target_pairs={{1,0},{2,1},{3,2},{4,3},{5,4},{6,5},{7,6},{9,8},{10,9},{11,10},{12... | collective-permute-start | bytes 196616 | tf_op jit(solution)/shard_map/ppermute | solution.py:23
  122.0 94.9 %all-reduce.5.cloned.1.call-start = ((), (), s32[]{:S(2)}) async-start(), calls=%async_computation.2 | async-start | bytes 884736 | tf_op jit(solution)/shard_map/psum | solution.py:101
  167.2 51.5 %copy-start.4 = (f32[256]{0:T(256)}, f32[256]{0:T(256)S(1)}, u32[]{:S(2)}) copy-start(f32[256]{0:T(256)S(1)} %get-tuple-element.97) | copy-start | bytes 3076
  167.2 51.5 %copy-start.5 = (f32[256]{0:T(256)}, f32[256]{0:T(256)S(1)}, u32[]{:S(2)}) copy-start(f32[256]{0:T(256)S(1)} %get-tuple-element.98) | copy-start | bytes 3076
Sparse Core Ops, SparseCore 0:
  122.1 48.3 reduce-scatter.1
  173.8 43.0 all-reduce.4
where the time goes:
time: 226 us
  blocking collectives  129 us (57%)
  waiting for transfers between devices  55.6 us (25%)
  between operations  14.5 us (6%)
  starting transfers between devices  12.6 us (6%)
  local copies, waits for them, and re-layouts  6.15 us (3%)
  other arithmetic  5.25 us (2%)
    psum x1, blocking collectives, shards(): lax.psum((jnp.sum(activation_grad * normed, axis=(0, 1, 2)), jnp.sum(acti...  45.1 us
    psum x1, waiting for transfers between devices, shards(): weight_grad = lax.psum(space_shard, 'tm')  45.1 us
    psum x1, blocking collectives, shards(): lax.psum(jnp.sum(values, axis=(0, 1, 2, 4)), ('tm', 'space')) / group_count  43.2 us
    psum x1, blocking collectives, shards(): lax.psum(jnp.sum(centered * centered, axis=(0, 1, 2, 4)), ('tm', 'space'))  41 us
    ppermute x4, starting transfers between devices, shifted(): lax.ppermute(value, axis, [(source, source + steps) for source in range(l...  9.8 us
    ppermute x1, waiting for transfers between devices, extended_2(): lax.ppermute(lax.slice_in_dim(block, 0, width, axis=dim), axis, backward)  4.55 us
  transfers between devices with their start and end apart: 8, of which 5 were waited for; matrix products, arithmetic and copies ran while one was open for 2% of the time, Pallas kernels for 0%

commit v1 on v0

--- a/solution.py
+++ b/solution.py
@@ -72,7 +72,8 @@
     group_mean = lax.psum(jnp.sum(values, axis=(0, 1, 2, 4)), ("tm", "space")) / group_count
     centered = values - group_mean[:, None]
     group_var = (
-        lax.psum(jnp.sum(centered * centered, axis=(0, 1, 2, 4)), ("tm", "space")) / group_count
+        lax.psum(lax.psum(jnp.sum(centered * centered, axis=(0, 1, 2, 4)), "space"), "tm")
+        / group_count
     )
     inv_std = lax.rsqrt(group_var + 1e-06)
     normed = (centered * inv_std[:, None]).reshape(frame_count, row_count, col_count, channels)

time: 226 us -> 205 us (0.907)
  blocking collectives: 129 us -> 112 us
    psum x1 -> x2, blocking collectives: 41 us -> 24.1 us  [the longest x1 14.4 us: shards(): lax.psum(jnp.sum(centered * centered, axis=(0, 1, 2, 4)), 'space')]
where the time goes in v1:
time: 205 us
  blocking collectives  112 us (55%)
  waiting for transfers between devices  55.5 us (27%)
  between operations  14.5 us (7%)
  starting transfers between devices  10.9 us (5%)
  local copies, waits for them, and re-layouts  5.95 us (3%)
  other arithmetic  4.4 us (2%)
  matrix products  2.07 us (1%)
    psum x1, waiting for transfers between devices, shards(): weight_grad = lax.psum(space_shard, 'tm')  45.1 us
    psum x1, blocking collectives, shards(): lax.psum((jnp.sum(activation_grad * normed, axis=(0, 1, 2)), jnp.sum(acti...  44.3 us
    psum x1, blocking collectives, shards(): lax.psum(jnp.sum(values, axis=(0, 1, 2, 4)), ('tm', 'space')) / group_count  43.2 us
    psum x1, blocking collectives, shards(): lax.psum(jnp.sum(centered * centered, axis=(0, 1, 2, 4)), 'space')  14.4 us
    psum x1, blocking collectives, shards(): lax.psum(lax.psum(jnp.sum(centered * centered, axis=(0, 1, 2, 4)), 'space...  9.73 us
    ppermute x4, starting transfers between devices, shifted(): lax.ppermute(value, axis, [(source, source + steps) for source in range(l...  8.06 us
    ppermute x1, waiting for transfers between devices, extended_2(): lax.ppermute(lax.slice_in_dim(block, 0, width, axis=dim), axis, backward)  4.55 us
  transfers between devices with their start and end apart: 8, of which 5 were waited for; matrix products, arithmetic and copies ran while one was open for 2% of the time, Pallas kernels for 0%

profile of v1, /device:TPU:0, one launch (start us, length us, event | category | flops | bytes accessed | tf_op | source)
XLA Modules:
  0.0 204.8 jit_solution(4642453897287166985)
XLA Ops:
  7.2 0.0 reduce-scatter.2.cloned.1.call-start
  7.2 0.9 convert_reduce_fusion
  8.1 0.1 reduce_sum.69
  8.2 0.1 reduce_sum.70
  8.3 1.3 collective-permute-start
  9.6 43.2 %psum.42 = f32[32]{0:T(128)S(1)} all-reduce(f32[32]{0:T(128)S(1)} %reduce_sum.70), channel_id=1, replica_groups=mesh['tm'=4,'space'=8] {'tm','space'}, use_global_device_ids=true, to_apply=%region_2.0 | all-reduce | flops 32 | bytes 256 | tf_op jit(solution)/shard_map/psum | solution.py:72
  52.8 0.1 sub.35
  52.8 0.1 sub.36
  52.9 0.0 copy-start
  52.9 1.6 fusion.40
  54.6 0.1 reduce_sum.72
  54.6 0.1 reduce_sum.73
  54.8 0.3 copy.15
  55.0 0.0 copy-start.1
  55.0 0.2 copy.13
  55.3 0.2 copy.14
  55.5 14.4 %psum.43 = f32[32]{0:T(128)S(1)} all-reduce(f32[32]{0:T(128)S(1)} %reduce_sum.73), channel_id=1, replica_groups=mesh['tm'=4,'space'=8] {'space'}, use_global_device_ids=true, to_apply=%region_5.6 | all-reduce | flops 32 | bytes 256 | tf_op jit(solution)/shard_map/psum | solution.py:75
  70.0 9.7 %psum.44 = f32[32]{0:T(128)S(1)} all-reduce(f32[32]{0:T(128)S(1)} %psum.43), channel_id=1, replica_groups=mesh['tm'=4,'space'=8] {'tm'}, use_global_device_ids=true, to_apply=%region_6.7 | all-reduce | flops 32 | bytes 256 | tf_op jit(solution)/shard_map/psum | solution.py:75
  79.8 0.1 constant_dynamic-update-slice_fusion.25
  79.9 0.1 constant_dynamic-update-slice_fusion.24
  79.9 0.1 constant_dynamic-update-slice_fusion.23
  80.0 0.1 constant_dynamic-update-slice_fusion.22
  80.1 0.1 constant_dynamic-update-slice_fusion.21
  80.1 0.1 constant_dynamic-update-slice_fusion.20
  80.2 0.1 constant_dynamic-update-slice_fusion.19
  80.3 0.1 constant_dynamic-update-slice_fusion.18
  80.4 0.3 fusion.42
  80.7 0.3 convolution_add_fusion.1
  81.1 0.0 copy-start.2
  81.1 0.0 copy-start.3
  81.1 0.3 convolution_add_fusion
  81.5 1.3 collective-permute-start.1
  82.8 0.1 mul.75
  82.9 0.1 mul.76
  83.0 3.0 %collective-permute-start.2 = (f32[2,32,256]{2,1,0:T(8,128)S(1)}, f32[2,32,256]{2,1,0:T(8,128)S(1)}, u32[]{:S(2)}, u32[]{:S(2)}) collective-permute-start(f32[2,32,256]{2,1,0:T(8,128)S(1)} %get-tuple-element.53), channel_id=1, source_target_pairs={{0,1},{1,2},{2,3},{3,4},{4,5},{5,6},{6,7},{8,9},{9,10},{10,11},{11... | collective-permute-start | bytes 196616 | tf_op jit(solution)/shard_map/ppermute | solution.py:12
  86.0 0.0 collective-permute-done.1
  86.0 0.9 collective-permute-done.2
  86.9 0.1 fusion.38
  87.0 2.4 %collective-permute-start.3 = (bf16[2,2,32,256]{3,2,1,0:T(8,128)(2,1)S(1)}, bf16[2,2,32,256]{3,2,1,0:T(8,128)(2,1)S(1)}, u32[]{:S(2)}, u32[]{:S(2)}) collective-permute-start(bf16[2,2,32,256]{3,2,1,0:T(8,128)(2,1)S(1)} %get-tuple-element.90), channel_id=1, source_target_pairs={{0,8},{8,16},{16,24},{1,9},{9,17},{17,25},{2,10},{10,18},{18,26},{... | collective-permute-start | bytes 196616 | tf_op jit(solution)/shard_map/ppermute | solution.py:12
  89.5 1.9 collective-permute-done.3
  91.4 1.4 collective-permute-start.4
  92.9 1.3 collective-permute-start.5
  94.2 4.6 %collective-permute-done.5 = bf16[4,1,32,256]{3,2,1,0:T(8,128)(2,1)S(1)} collective-permute-done((bf16[4,1,32,256]{3,2,1,0:T(8,128)(2,1)S(1)}, bf16[4,1,32,256]{3,2,1,0:T(8,128)(2,1)S(1)}, u32[]{:S(2)}, u32[]{:S(2)}) %collective-permute-start.5) | collective-permute-done | bytes 65568 | tf_op jit(solution)/shard_map/ppermute | solution.py:23
  98.8 0.1 select_maximum_fusion
  99.2 0.3 convolution_bitcast_fusion
  99.6 0.3 convolution_bitcast_fusion.2
  99.9 0.3 convolution_bitcast_fusion.1
  100.3 2.0 pad_maximum_fusion
  102.3 0.0 reduce-scatter.2.cloned.1.call-update
  102.3 0.0 all-reduce.5.cloned.1.call-start
  102.3 44.3 %all-reduce.2 = (f32[256]{0:T(256)S(1)}, f32[256]{0:T(256)S(1)}) all-reduce(f32[256]{0:T(256)S(1)} %get-tuple-element.29, f32[256]{0:T(256)S(1)} %get-tuple-element.28), channel_id=1, replica_groups=mesh['tm'=4,'space'=8] {'tm','space'}, use_global_device_ids=true, to_apply=%region_11.12 | all-reduce | flops 512 | bytes 4096 | tf_op jit(solution)/shard_map/psum | solution.py:111
  146.6 0.1 reshape.151
  146.7 0.1 reduce_sum.75
  146.8 3.0 %reduce-scatter.2.cloned.1.call-done = f32[864,128]{1,0:T(8,128)} async-done(((f32[6912,128]{1,0:T(8,128)}), f32[864,128]{1,0:T(8,128)}) %reduce-scatter.2.cloned.1.call-update) | async-done | bytes 442384 | tf_op jit(solution)/shard_map/reduce_scatter | solution.py:101
  149.8 0.0 all-reduce.5.cloned.1.call-update
  149.9 0.1 sub.40
  149.9 0.1 sub.41
  150.0 0.1 reshape.152
  150.1 0.1 reduce_sum.77
  150.2 0.1 mul.88
  150.3 0.1 mul.89
  150.4 0.7 fusion.32
  151.1 45.1 %all-reduce.5.cloned.1.call-done = f32[864,128]{1,0:T(8,128)} async-done(((f32[864,128]{1,0:T(8,128)}), f32[864,128]{1,0:T(8,128)}) %all-reduce.5.cloned.1.call-update) | async-done | bytes 442384 | tf_op jit(solution)/shard_map/psum | solution.py:102
  196.2 1.8 copy.74
  (36 shorter events, 0.5 us)
Async XLA Ops:
  7.2 142.7 %reduce-scatter.2.cloned.1.call-start = ((), (), s32[]{:S(2)}) async-start(), calls=%async_computation.1 | async-start | bytes 3981312 | tf_op jit(solution)/shard_map/reduce_scatter | solution.py:101
  8.3 71.4 %collective-permute-start = (bf16[2,2,32,128]{3,2,1,0:T(8,128)(2,1)}, bf16[2,2,32,128]{3,2,1,0:T(8,128)(2,1)S(1)}, u32[]{:S(2)}, u32[]{:S(2)}) collective-permute-start(bf16[2,2,32,128]{3,2,1,0:T(8,128)(2,1)} %param.10), channel_id=1, source_target_pairs={{8,0},{16,8},{24,16},{9,1},{17,9},{25,17},{10,2},{18,10},{26,18},{... | collective-permute-start | bytes 98312 | tf_op jit(solution)/shard_map/ppermute | solution.py:12
  52.9 1.6 copy-start
  55.0 24.7 %copy-start.1 = (bf16[2,2,32,128]{3,2,1,0:T(8,128)(2,1)S(1)}, bf16[2,2,32,128]{3,2,1,0:T(8,128)(2,1)}, u32[]{:S(2)}) copy-start(bf16[2,2,32,128]{3,2,1,0:T(8,128)(2,1)} %param.10) | copy-start | bytes 98308
  81.1 5.8 %copy-start.2 = (f32[256]{0:T(256)S(1)}, f32[256]{0:T(256)}, u32[]{:S(2)}) copy-start(f32[256]{0:T(256)} %param.12) | copy-start | bytes 3076
  81.1 5.8 %copy-start.3 = (f32[256]{0:T(256)S(1)}, f32[256]{0:T(256)}, u32[]{:S(2)}) copy-start(f32[256]{0:T(256)} %param.13) | copy-start | bytes 3076
  81.5 4.5 %collective-permute-start.1 = (f32[2,32,256]{2,1,0:T(8,128)S(1)}, f32[2,32,256]{2,1,0:T(8,128)S(1)}, u32[]{:S(2)}, u32[]{:S(2)}) collective-permute-start(f32[2,32,256]{2,1,0:T(8,128)S(1)} %get-tuple-element.54), channel_id=1, source_target_pairs={{1,0},{2,1},{3,2},{4,3},{5,4},{6,5},{7,6},{9,8},{10,9},{11,10},{12... | collective-permute-start | bytes 196616 | tf_op jit(solution)/shard_map/ppermute | solution.py:12
  83.0 3.9 %collective-permute-start.2 = (f32[2,32,256]{2,1,0:T(8,128)S(1)}, f32[2,32,256]{2,1,0:T(8,128)S(1)}, u32[]{:S(2)}, u32[]{:S(2)}) collective-permute-start(f32[2,32,256]{2,1,0:T(8,128)S(1)} %get-tuple-element.53), channel_id=1, source_target_pairs={{0,1},{1,2},{2,3},{3,4},{4,5},{5,6},{6,7},{8,9},{9,10},{10,11},{11... | collective-permute-start | bytes 196616 | tf_op jit(solution)/shard_map/ppermute | solution.py:12
  87.0 4.4 %collective-permute-start.3 = (bf16[2,2,32,256]{3,2,1,0:T(8,128)(2,1)S(1)}, bf16[2,2,32,256]{3,2,1,0:T(8,128)(2,1)S(1)}, u32[]{:S(2)}, u32[]{:S(2)}) collective-permute-start(bf16[2,2,32,256]{3,2,1,0:T(8,128)(2,1)S(1)} %get-tuple-element.90), channel_id=1, source_target_pairs={{0,8},{8,16},{16,24},{1,9},{9,17},{17,25},{2,10},{10,18},{18,26},{... | collective-permute-start | bytes 196616 | tf_op jit(solution)/shard_map/ppermute | solution.py:12
  91.4 2.8 %collective-permute-start.4 = (bf16[4,1,32,256]{3,2,1,0:T(8,128)(2,1)S(1)}, bf16[4,1,32,256]{3,2,1,0:T(8,128)(2,1)S(1)}, u32[]{:S(2)}, u32[]{:S(2)}) collective-permute-start(bf16[4,1,32,256]{3,2,1,0:T(8,128)(2,1)S(1)} %get-tuple-element.88), channel_id=1, source_target_pairs={{0,1},{1,2},{2,3},{3,4},{4,5},{5,6},{6,7},{8,9},{9,10},{10,11},{11... | collective-permute-start | bytes 196616 | tf_op jit(solution)/shard_map/ppermute | solution.py:20
  92.9 5.9 %collective-permute-start.5 = (bf16[4,1,32,256]{3,2,1,0:T(8,128)(2,1)S(1)}, bf16[4,1,32,256]{3,2,1,0:T(8,128)(2,1)S(1)}, u32[]{:S(2)}, u32[]{:S(2)}) collective-permute-start(bf16[4,1,32,256]{3,2,1,0:T(8,128)(2,1)S(1)} %get-tuple-element.89), channel_id=1, source_target_pairs={{1,0},{2,1},{3,2},{4,3},{5,4},{6,5},{7,6},{9,8},{10,9},{11,10},{12... | collective-permute-start | bytes 196616 | tf_op jit(solution)/shard_map/ppermute | solution.py:23
  102.3 93.9 %all-reduce.5.cloned.1.call-start = ((), (), s32[]{:S(2)}) async-start(), calls=%async_computation.2 | async-start | bytes 884736 | tf_op jit(solution)/shard_map/psum | solution.py:102
  146.6 51.4 %copy-start.4 = (f32[256]{0:T(256)}, f32[256]{0:T(256)S(1)}, u32[]{:S(2)}) copy-start(f32[256]{0:T(256)S(1)} %get-tuple-element.97) | copy-start | bytes 3076
  146.6 51.4 %copy-start.5 = (f32[256]{0:T(256)}, f32[256]{0:T(256)S(1)}, u32[]{:S(2)}) copy-start(f32[256]{0:T(256)S(1)} %get-tuple-element.98) | copy-start | bytes 3076
Sparse Core Ops, SparseCore 0:
  102.4 47.3 reduce-scatter.1
  153.1 43.0 all-reduce.4
